TPU v7x, 256 devices: a whole 4x4x8 slice. The times are simulated.
256 devices in a mesh: wide: 32 (over z, y_hi, core), narrow: 8 (over y_lo, x).
Axes of the slice: x: 4, y: 4 (y_hi: 2, y_lo: 2; y = y_hi * 2 + y_lo), z: 8, core: 2. Of those that a mesh axis runs over, the one named last changes fastest.
Arguments:
- buoyancy: float32 [512, 512, 128], P('wide', 'narrow'), may hold values from -6 to 6
- velocity_x: float32 [512, 512, 128], P('wide', 'narrow'), may hold values from -0.0078125 to 0.0078125
- velocity_y: float32 [512, 512, 128], P('wide', 'narrow'), may hold values from -0.0078125 to 0.0078125
- velocity_z: float32 [512, 512, 128], P('wide', 'narrow'), may hold values from -0.0078125 to 0.0078125
- inverse_blocks: bfloat16 [256, 256, 128, 128], P('wide', 'narrow'), may hold values from -1 to 2, as said below
Outputs:
- new_buoyancy: float32 [512, 512, 128], P('wide', 'narrow')
Inputs may be any that keep to these rules, and one draw needn't show every extreme that they name: `inverse_blocks`: dense 128 x 128 blocks, one for each pair of x and y mode numbers.
All inputs are finite; a program needn't handle non-finite values.
Results may differ from a plain program's by a relative error of at most 0.0029.
Values sent between devices are 32-bit elements; how exact they have to be, the bound alone decides.
A program may use at most 128 MiB of HBM per device.

v0:
```python
import math

import jax
import jax.numpy as jnp
from jax import lax
from jax.sharding import PartitionSpec as P

NX = 512
NY = 512
NZ = 128
MX = 768
MY = 768
MZ = 192


HIGHEST = lax.Precision.HIGHEST


def fourier_table(n_coef, n_grid):
    coef_index = jnp.arange(n_coef)
    modes = coef_index // 2
    points = jnp.arange(n_grid)
    phase = (modes[:, None] * points[None, :] % n_grid).astype(jnp.float32) * (
        2.0 * math.pi / n_grid
    )
    return jnp.where((coef_index % 2 == 0)[:, None], jnp.cos(phase), jnp.sin(phase))


def fourier_inverse(n_coef, n_grid):
    coef_index = jnp.arange(n_coef)
    modes = coef_index // 2
    weight = jnp.where(modes == 0, jnp.where(coef_index % 2 == 0, 1.0 / n_grid, 0.0), 2.0 / n_grid)
    return fourier_table(n_coef, n_grid).T * weight.astype(jnp.float32)[None, :]


def cheb_table(n_coef, n_grid):
    orders = jnp.arange(n_coef)
    points = jnp.arange(n_grid)
    index_grid = orders[:, None] * (2 * points[None, :] + 1) % (4 * n_grid)
    return jnp.cos(index_grid.astype(jnp.float32) * (math.pi / (2 * n_grid)))


def cheb_inverse(n_coef, n_grid):
    orders = jnp.arange(n_coef)
    weight = jnp.where(orders == 0, 1.0 / n_grid, 2.0 / n_grid).astype(jnp.float32)
    return cheb_table(n_coef, n_grid).T * weight[None, :]


def cheb_slope(n_coef):
    rows = jnp.arange(n_coef)[:, None]
    cols = jnp.arange(n_coef)[None, :]
    inside = (cols > rows) & ((cols - rows) % 2 == 1)
    factor = jnp.where(rows == 0, 1.0, 2.0) * cols
    return jnp.where(inside, factor, 0.0).astype(jnp.float32)


def fourier_slope(values, axis_pos, start):
    shape = values.shape
    count = shape[axis_pos]
    paired = values.reshape(shape[:axis_pos] + (count // 2, 2) + shape[axis_pos + 1 :])
    cosines = lax.index_in_dim(paired, 0, axis_pos + 1, keepdims=False)
    sines = lax.index_in_dim(paired, 1, axis_pos + 1, keepdims=False)
    modes = (start // 2 + jnp.arange(count // 2)).astype(jnp.float32)
    modes = modes.reshape((count // 2,) + (1,) * (len(shape) - axis_pos - 1))
    return jnp.stack([modes * sines, -modes * cosines], axis=axis_pos + 1).reshape(shape)


def per_device(buoyancy, velocity_x, velocity_y, velocity_z, inverse_blocks):
    x_local, y_local, depth = buoyancy.shape
    wide_count = lax.axis_size("wide")
    narrow_count = lax.axis_size("narrow")
    x_start = lax.axis_index("wide") * x_local
    y_start = lax.axis_index("narrow") * y_local
    x_forward = fourier_table(NX, MX)
    y_forward = fourier_table(NY, MY)
    z_forward = cheb_table(NZ, MZ)
    x_backward = fourier_inverse(NX, MX)
    y_backward = fourier_inverse(NY, MY)
    z_backward = cheb_inverse(NZ, MZ)
    z_slope = cheb_slope(NZ)
    fields = jnp.stack([velocity_x, velocity_y, velocity_z, buoyancy])
    along_z = jnp.einsum("fayn,nq->fqay", fields, z_forward, precision=HIGHEST)
    along_z = along_z.reshape(4, MZ, 1, x_local * y_local)
    q_part = MZ // narrow_count
    j_part = MY // wide_count
    incoming = lax.all_to_all(along_z, "narrow", split_axis=1, concat_axis=2, tiled=True)
    items = incoming.shape[0]
    split = incoming.reshape(items, q_part, narrow_count, x_local, y_local)
    table = y_forward.reshape(narrow_count, y_local, MY)
    result = jnp.einsum("fqsay,syj->fjqa", split, table, precision=HIGHEST)
    along_y = result.reshape(items, 1, MY, q_part * x_local)
    incoming = lax.all_to_all(along_y, "wide", split_axis=2, concat_axis=1, tiled=True)
    items = incoming.shape[0]
    split = incoming.reshape(items, wide_count, j_part, q_part, x_local)
    table = x_forward.reshape(wide_count, x_local, MX)
    grid = jnp.einsum("fsjqa,sap->fjqp", split, table, precision=HIGHEST)
    fluxes = grid[:3] * grid[3:4]
    x_coef = jnp.einsum("fjqp,pa->faqj", fluxes, x_backward, precision=HIGHEST)
    x_coef = x_coef.reshape(3, NX, 1, q_part * j_part)
    incoming = lax.all_to_all(x_coef, "wide", split_axis=1, concat_axis=2, tiled=True)
    items = incoming.shape[0]
    split = incoming.reshape(items, x_local, wide_count, q_part, j_part)
    table = y_backward.reshape(wide_count, j_part, NY)
    result = jnp.einsum("fasqj,sjy->fyaq", split, table, precision=HIGHEST)
    y_coef = result.reshape(items, NY, 1, x_local * q_part)
    incoming = lax.all_to_all(y_coef, "narrow", split_axis=1, concat_axis=2, tiled=True)
    items = incoming.shape[0]
    split = incoming.reshape(items, y_local, narrow_count, x_local, q_part)
    table = z_backward.reshape(narrow_count, q_part, NZ)
    coefs = jnp.einsum("fysaq,sqn->fayn", split, table, precision=HIGHEST)
    vertical = jnp.einsum("ayp,np->ayn", coefs[2], z_slope, precision=HIGHEST)
    nonlinear = fourier_slope(coefs[0], 0, x_start) + fourier_slope(coefs[1], 1, y_start) + vertical
    right_side = (buoyancy - 4.0 / NX * nonlinear).astype(jnp.bfloat16)
    grouped = right_side.reshape(x_local // 2, 2, y_local // 2, 2, depth)
    solved = jnp.einsum(
        "xyin,xaybn->xaybi", inverse_blocks, grouped, preferred_element_type=jnp.float32
    )
    return solved.reshape(x_local, y_local, depth)


def solution(mesh):
    placed = (
        P("wide", "narrow", None),
        P("wide", "narrow", None),
        P("wide", "narrow", None),
        P("wide", "narrow", None),
        P("wide", "narrow", None, None),
    )
    return jax.shard_map(
        per_device, mesh=mesh, in_specs=placed, out_specs=P("wide", "narrow", None), check_vma=False
    )
```

profile of v0, /device:TPU:1, one launch (start us, length us, event | category | flops | bytes accessed | tf_op | source)
XLA Modules:
  0.0 653.4 jit_solution(815738947671382957)
XLA Ops:
  0.0 7.3 %fusion.9 = f32[192,4,16,64]{0,3,2,1:T(8,128)} fusion(f32[1,16,64,128]{3,2,1,0:T(8,128)} %bitcast.131, f32[1,16,64,128]{3,2,1,0:T(8,128)} %bitcast.133, f32[1,16,64,128]{3,2,1,0:T(8,128)} %bitcast.134, f32[1,16,64,128]{3,2,1,0:T(8,128)} %bitcast.135, s32[192]{0:T(256)S(1)} %multiply_add_fusion.4), kind=kOutput, calls=%fused_computation.13 | convolution fusion | flops 1209753600 | bytes 5243648 | tf_op jit(solution)/shard_map/fayn,nq->fqay/dot_general | solution.py:82
  7.3 5.1 copy.55
  12.4 5.9 all-to-all-start
  18.3 38.3 %all-to-all-done = f32[4,192,1,1024]{3,0,2,1:T(4,128)S(1)} async-done(((f32[4,192,1,1024]{3,0,2,1:T(4,128)}), f32[4,192,1,1024]{3,0,2,1:T(4,128)S(1)}, u32[]{:S(2)}, u32[]{:S(2)}) %all-to-all-start) | async-done | bytes 3145760 | tf_op jit(solution)/shard_map/all_to_all | solution.py:86
  56.5 3.5 copy.56
  60.1 5.7 reshape.283
  65.8 24.7 %fusion.6 = f32[4,768,24,16]{1,2,3,0:T(8,128)S(1)} fusion(f32[4,24,8,16,64]{4,3,1,2,0:T(8,128)} %reshape.283, s32[8,64]{1,0:T(8,128)S(1)} %add_select_fusion.9, pred[8,64]{1,0:T(8,128)(4,1)S(1)} %fusion.148), kind=kOutput, calls=%fused_computation.12 | convolution fusion | flops 7251689472 | bytes 7866880 | tf_op jit(solution)/shard_map/fqsay,syj->fjqa/dot_general | solution.py:90
  90.5 3.6 copy.59
  94.0 6.7 %copy.60 = f32[4,1,768,384]{3,0,1,2:T(4,128)} copy(f32[4,1,768,384]{2,3,0,1:T(8,128)} %bitcast.119) | data formatting | bytes 9437184 | tf_op jit(solution)/shard_map/reshape | solution.py:91
  100.7 11.9 %all-to-all-start.1 = ((f32[4,1,768,384]{3,0,1,2:T(4,128)}), f32[4,1,768,384]{3,0,1,2:T(4,128)}, u32[]{:S(2)}, u32[]{:S(2)}) async-start(f32[4,1,768,384]{3,0,1,2:T(4,128)} %copy.60), calls=%async_computation.1 | async-start | bytes 9437184 | tf_op jit(solution)/shard_map/all_to_all | solution.py:92
  112.7 105.1 %all-to-all-done.1 = f32[4,1,768,384]{3,0,1,2:T(4,128)} async-done(((f32[4,1,768,384]{3,0,1,2:T(4,128)}), f32[4,1,768,384]{3,0,1,2:T(4,128)}, u32[]{:S(2)}, u32[]{:S(2)}) %all-to-all-start.1) | async-done | bytes 4718624 | tf_op jit(solution)/shard_map/all_to_all | solution.py:92
  217.8 6.7 %copy.61 = f32[4,1,768,384]{2,3,0,1:T(8,128)} copy(f32[4,1,768,384]{3,0,1,2:T(4,128)} %all-to-all-done.1) | data formatting | bytes 9437184 | tf_op jit(solution)/shard_map/all_to_all | solution.py:92
  224.5 20.6 %reshape.262 = f32[4,32,24,24,16]{2,1,4,3,0:T(8,128)} reshape(f32[4,1,768,384]{2,3,0,1:T(8,128)} %copy.61) | data formatting | bytes 9437184 | tf_op jit(solution)/shard_map/reshape | solution.py:94
  245.1 140.7 %convolution_bitcast_fusion = f32[4,24,24,768]{3,1,2,0:T(8,128)} fusion(f32[4,32,24,24,16]{2,1,4,3,0:T(8,128)} %reshape.262, s32[32,16]{0,1:T(8,128)S(1)} %add_select_fusion.7, pred[32,16]{0,1:T(8,128)(4,1)S(1)} %fusion.142), kind=kOutput, calls=%fused_computation.7 | convolution fusion | flops 10875568128 | bytes 11799040 | tf_op jit(solution)/shard_map/fsjqa,sap->fjqp/dot_general | solution.py:96
  385.9 1.6 slice_bitcast_fusion
  387.5 3.0 slice_multiply_fusion
  390.4 16.1 %fusion.17 = f32[3,512,24,24]{1,2,3,0:T(8,128)S(1)} fusion(f32[3,24,24,768]{3,1,2,0:T(8,128)S(1)} %slice_multiply_fusion, f32[512]{0:T(512)S(1)} %select_select_fusion, s32[512]{0:T(512)S(1)} %add_select_fusion.11, pred[512]{0:T(512)(128)(4,1)S(1)} %fusion.154), kind=kOutput, calls=%fused_computation.21 | convolution fusion | flops 8158052352 | bytes 8851968 | tf_op jit(solution)/shard_map/fjqp,pa->faqj/dot_general | solution.py:98
  406.6 2.1 copy.64
  408.6 6.1 copy.65
  414.7 7.6 %all-to-all-start.2 = ((f32[3,512,1,576]{3,2,0,1:T(1,128)}), f32[3,512,1,576]{3,2,0,1:T(1,128)}, u32[]{:S(2)}, u32[]{:S(2)}) async-start(f32[3,512,1,576]{3,2,0,1:T(1,128)} %copy.65), calls=%async_computation.2 | async-start | bytes 7864320 | tf_op jit(solution)/shard_map/all_to_all | solution.py:100
  422.4 91.0 %all-to-all-done.2 = f32[3,512,1,576]{3,2,0,1:T(1,128)} async-done(((f32[3,512,1,576]{3,2,0,1:T(1,128)}), f32[3,512,1,576]{3,2,0,1:T(1,128)}, u32[]{:S(2)}, u32[]{:S(2)}) %all-to-all-start.2) | async-done | bytes 3538976 | tf_op jit(solution)/shard_map/all_to_all | solution.py:100
  513.3 4.3 copy.66
  517.7 12.8 %reshape.284 = f32[3,16,32,24,24]{4,3,1,2,0:T(8,128)} reshape(f32[3,16,32,1,576]{4,1,2,0,3:T(8,128)} %bitcast.121) | data formatting | bytes 7077888 | tf_op jit(solution)/shard_map/reshape | solution.py:102
  530.4 18.3 %copy.68 = f32[3,16,32,24,24]{2,3,4,1,0:T(8,128)} copy(f32[3,16,32,24,24]{4,3,1,2,0:T(8,128)} %reshape.284) | data formatting | bytes 7077888 | tf_op jit(solution)/shard_map/reshape | solution.py:102
  548.7 34.9 %fusion.31 = f32[512,3,16,24,1]{0,3,4,2,1:T(8,128)S(1)} fusion(f32[3,16,32,24,24]{2,3,4,1,0:T(8,128)} %copy.68, f32[512]{0:T(512)S(1)} %select_select_fusion, s32[32,24]{0,1:T(8,128)S(1)} %multiply_add_fusion, s32[512]{0:T(512)S(1)} %add_select_fusion.11, pred[512]{0:T(512)(128)(4,1)S(1)} %fusion.154), kind=kOutput, calls=%fused_computation.34 | convolution fusion | flops 5440143360 | bytes 5905920 | tf_op jit(solution)/shard_map/fasqj,sjy->fyaq/dot_general | solution.py:104
  583.7 4.6 copy.69
  588.3 11.1 %all-to-all-start.3 = ((f32[3,512,1,384]{3,2,0,1:T(1,128)}), f32[3,512,1,384]{3,2,0,1:T(1,128)}, u32[]{:S(2)}, u32[]{:S(2)}) async-start(f32[3,512,1,384]{3,2,0,1:T(1,128)} %copy.69), calls=%async_computation.3 | async-start | bytes 4718592 | tf_op jit(solution)/shard_map/all_to_all | solution.py:106
  599.4 29.9 %all-to-all-done.3 = f32[3,512,1,384]{3,2,0,1:T(1,128)} async-done(((f32[3,512,1,384]{3,2,0,1:T(1,128)}), f32[3,512,1,384]{3,2,0,1:T(1,128)}, u32[]{:S(2)}, u32[]{:S(2)}) %all-to-all-start.3) | async-done | bytes 2359328 | tf_op jit(solution)/shard_map/all_to_all | solution.py:106
  629.3 1.8 copy.70
  631.2 3.4 copy.71
  634.6 0.0 slice-start
  634.6 10.2 %convolution_bitcast_fusion.1 = f32[3,16,64,128]{3,2,1,0:T(8,128)S(1)} fusion(f32[3,64,8,16,24]{1,4,3,2,0:T(8,128)} %bitcast.118, f32[128]{0:T(128)S(1)} %compare_select_fusion.1, s32[8,24]{1,0:T(8,128)S(1)} %multiply_add_fusion.3), kind=kOutput, calls=%fused_computation.66 | convolution fusion | flops 906215424 | bytes 3933440 | tf_op jit(solution)/shard_map/fysaq,sqn->fayn/dot_general | solution.py:110
  644.8 0.0 slice-start.1
  644.8 0.1 fusion.185
  644.9 0.6 slice_multiply_fusion.2
  645.5 0.5 pad_maximum_fusion.1
  645.9 0.1 slice_multiply_fusion.4
  646.0 0.0 copy-start
  646.1 0.1 bitcast_add_fusion
  646.2 0.9 copy-done
  647.1 0.7 fusion.72
  647.8 0.0 slice-done
  647.8 0.0 slice-done.1
  647.8 4.4 fusion.67
  652.2 1.0 copy.74
  (19 shorter events, 0.2 us)
Async XLA Ops:
  12.4 44.1 %all-to-all-start = ((f32[4,192,1,1024]{3,0,2,1:T(4,128)}), f32[4,192,1,1024]{3,0,2,1:T(4,128)S(1)}, u32[]{:S(2)}, u32[]{:S(2)}) async-start(f32[4,192,1,1024]{3,0,2,1:T(4,128)} %copy.55), calls=%async_computation | async-start | bytes 6291456 | tf_op jit(solution)/shard_map/all_to_all | solution.py:86
  100.7 117.1 %all-to-all-start.1 = ((f32[4,1,768,384]{3,0,1,2:T(4,128)}), f32[4,1,768,384]{3,0,1,2:T(4,128)}, u32[]{:S(2)}, u32[]{:S(2)}) async-start(f32[4,1,768,384]{3,0,1,2:T(4,128)} %copy.60), calls=%async_computation.1 | async-start | bytes 9437184 | tf_op jit(solution)/shard_map/all_to_all | solution.py:92
  414.7 98.6 %all-to-all-start.2 = ((f32[3,512,1,576]{3,2,0,1:T(1,128)}), f32[3,512,1,576]{3,2,0,1:T(1,128)}, u32[]{:S(2)}, u32[]{:S(2)}) async-start(f32[3,512,1,576]{3,2,0,1:T(1,128)} %copy.65), calls=%async_computation.2 | async-start | bytes 7864320 | tf_op jit(solution)/shard_map/all_to_all | solution.py:100
  588.3 41.1 %all-to-all-start.3 = ((f32[3,512,1,384]{3,2,0,1:T(1,128)}), f32[3,512,1,384]{3,2,0,1:T(1,128)}, u32[]{:S(2)}, u32[]{:S(2)}) async-start(f32[3,512,1,384]{3,2,0,1:T(1,128)} %copy.69), calls=%async_computation.3 | async-start | bytes 4718592 | tf_op jit(solution)/shard_map/all_to_all | solution.py:106
  634.6 13.2 %slice-start = ((s8[8388608]{0:T(1024)(128)(4,1)}), s8[4194304]{0:T(1024)(128)(4,1)S(1)}, s32[]{:S(2)}) async-start(s8[8388608]{0:T(1024)(128)(4,1)} %bitcast.125), calls=%async_computation.4 | async-start | bytes 8388608
  644.8 3.0 slice-start.1
  646.0 1.0 copy-start
where the time goes:
time: 663 us; the launch traced here: 653 us
  waiting for transfers between devices  264 us (40%)
  matrix products  239 us (36%)
  local copies, waits for them, and re-layouts  109 us (16%)
  starting transfers between devices  36.4 us (5%)
    dot_general x1, matrix products, per_device(): grid = jnp.einsum('fsjqa,sap->fjqp', split, table, precision=HIGHEST)  141 us
    all_to_all x1, waiting for transfers between devices, per_device(): lax.all_to_all(along_y, 'wide', split_axis=2, concat_axis=1, tiled=True)  105 us
    all_to_all x1, waiting for transfers between devices, per_device(): lax.all_to_all(x_coef, 'wide', split_axis=1, concat_axis=2, tiled=True)  91 us
    all_to_all x1, waiting for transfers between devices, per_device(): lax.all_to_all(along_z, 'narrow', split_axis=1, concat_axis=2, tiled=True)  38.3 us
    dot_general x1, matrix products, per_device(): result = jnp.einsum('fasqj,sjy->fyaq', split, table, precision=HIGHEST)  34.9 us
    reshape x2, local copies, waits for them, and re-layouts, per_device(): split = incoming.reshape(items, x_local, wide_count, q_part, j_part)  31.1 us
    all_to_all x1, waiting for transfers between devices, per_device(): lax.all_to_all(y_coef, 'narrow', split_axis=1, concat_axis=2, tiled=True)  29.9 us
    dot_general x1, matrix products, per_device(): result = jnp.einsum('fqsay,syj->fjqa', split, table, precision=HIGHEST)  24.7 us
  transfers between devices with their start and end apart: 4, of which 4 were waited for; matrix products, arithmetic and copies ran while one was open for 0% of the time, Pallas kernels for 0%

commit v1 on v0

v1 whole, which is shorter than its diff:
```python
import functools

import jax
import jax.numpy as jnp
import ml_dtypes
import numpy as np
from jax import lax
from jax.experimental import pallas as pl
from jax.experimental.pallas import tpu as pltpu
from jax.sharding import PartitionSpec as P

NX = 512
NY = 512
NZ = 128
MX = 768
MY = 768
MZ = 192
W = 32
N = 8
XL = NX // W
YL = NY // N
QL = MZ // W
PL = MX // N
PAIRS = QL // 2
F32 = jnp.float32
BF16 = jnp.bfloat16
MESH = pl.DeviceIdType.MESH


def fourier_table(n_coef, n_grid):
    index = np.arange(n_coef)
    phase = (index[:, None] // 2 * np.arange(n_grid)[None, :] % n_grid) * (2.0 * np.pi / n_grid)
    return np.where((index % 2 == 0)[:, None], np.cos(phase), np.sin(phase))


def fourier_inverse(n_coef, n_grid):
    index = np.arange(n_coef)
    modes = index // 2
    weight = np.where(modes == 0, np.where(index % 2 == 0, 1.0 / n_grid, 0.0), 2.0 / n_grid)
    return fourier_table(n_coef, n_grid).T * weight[None, :]


def fourier_inverse_slope(n_coef, n_grid):
    plain = fourier_inverse(n_coef, n_grid)
    modes = np.arange(n_coef // 2)[None, :]
    result = np.empty_like(plain)
    result[:, 0::2] = modes * plain[:, 1::2]
    result[:, 1::2] = -modes * plain[:, 0::2]
    return result


def cheb_table(n_coef, n_grid):
    orders = np.arange(n_coef)
    points = np.arange(n_grid)
    index_grid = orders[:, None] * (2 * points[None, :] + 1) % (4 * n_grid)
    return np.cos(index_grid * (np.pi / (2 * n_grid)))


def cheb_inverse(n_coef, n_grid):
    weight = np.where(np.arange(n_coef) == 0, 1.0 / n_grid, 2.0 / n_grid)
    return cheb_table(n_coef, n_grid).T * weight[None, :]


def cheb_slope(n_coef):
    rows = np.arange(n_coef)[:, None]
    cols = np.arange(n_coef)[None, :]
    inside = (cols > rows) & ((cols - rows) % 2 == 1)
    return np.where(inside, np.where(rows == 0, 1.0, 2.0) * cols, 0.0)


def split_table(table):
    high = table.astype(np.float32).astype(ml_dtypes.bfloat16)
    low = (table - high.astype(np.float64)).astype(np.float32).astype(ml_dtypes.bfloat16)
    return np.stack([high, low])


@functools.cache
def tables():
    z_forward = cheb_table(NZ, MZ).T.reshape(W, QL, NZ).transpose(1, 0, 2).reshape(MZ, NZ)
    x_forward = fourier_table(NX, MX).T
    y_forward = fourier_table(NY, MY)
    y_backward = fourier_inverse(NY, MY)
    y_slope = fourier_inverse_slope(NY, MY)
    x_backward = fourier_inverse(NX, MX).T
    x_slope = fourier_inverse_slope(NX, MX).T
    plain = cheb_inverse(NZ, MZ)
    sloped = plain @ cheb_slope(NZ).T
    sides = []
    for parity in range(2):
        blocks = []
        for half in range(2):
            parts = []
            for source in (plain, sloped):
                by_chunk = source.reshape(W, PAIRS, 2, NZ)[:, :, half ^ parity]
                parts.append(by_chunk.transpose(2, 1, 0).reshape(NZ, PAIRS * W))
            parts.append(np.zeros((NZ, 256 - 2 * PAIRS * W)))
            blocks.append(np.concatenate(parts, axis=1))
        sides.append(np.concatenate(blocks, axis=0))
    z_backward = np.stack(sides)
    return [
        split_table(t)
        for t in (z_forward, x_forward, y_forward, y_backward, y_slope, x_backward, x_slope, z_backward)
    ]


def halves(value):
    high = value.astype(BF16)
    return high, (value - high.astype(F32)).astype(BF16)


def dot(a, b, dims=((1,), (0,))):
    return lax.dot_general(a, b, (dims, ((), ())), preferred_element_type=F32)


def dot3(a_high, a_low, b_high, b_low):
    return dot(a_high, b_high) + dot(a_low, b_high) + dot(a_high, b_low)


def rows(start, size):
    return pl.ds(pl.multiple_of(start, 16), size)


def kernel(
    vx_ref, vy_ref, vz_ref, b_ref, zf, zb, xf_hbm, yf_hbm, yb_hbm, ys_hbm, xb_hbm, xs_hbm,
    out_ref,
    send1, recv1, send2, recv2, send3, recv3, send4, recv4,
    xf, yf, yb, ys, xb, xs,
    xh, xl, yh, yl, gh, gl, bh, bl, zh, zl,
    table_sem, s1, r1, s2, r2, s3, r3, s4, r4,
):
    w = lax.axis_index("wide")
    n = lax.axis_index("narrow")
    across = lax.rem(n + 4, N)
    parity = lax.rem(n, 2)
    z_pos, rest = w // 4, lax.rem(w, 4)
    y_pos, x_pos = n // 4, lax.rem(n, 4)

    def wide_peer(k):
        return lax.rem(z_pos + k // 4, 8) * 4 + lax.rem(rest + lax.rem(k, 4), 4)

    def narrow_peer(k):
        return lax.rem(y_pos + k // 4, 2) * 4 + lax.rem(x_pos + lax.rem(k, 4), 4)

    table_copies = [
        pltpu.make_async_copy(hbm, vmem, table_sem.at[i])
        for i, (hbm, vmem) in enumerate(
            ((xf_hbm, xf), (yf_hbm, yf), (yb_hbm, yb), (ys_hbm, ys), (xb_hbm, xb), (xs_hbm, xs))
        )
    ]
    for copy in table_copies:
        copy.start()

    barrier = pltpu.get_barrier_semaphore()

    @pl.loop(0, W)
    def _(k):
        pl.semaphore_signal(barrier, inc=1, device_id=(wide_peer(k), across), device_id_type=MESH)

    for k in (1, 2, 3, 5, 6, 7):
        pl.semaphore_signal(barrier, inc=1, device_id=(w, narrow_peer(k)), device_id_type=MESH)

    odd = parity == 1

    @pl.loop(0, XL)
    def _(a):
        vx, vy, vz, b = vx_ref[a], vy_ref[a], vz_ref[a], b_ref[a]
        data = jnp.concatenate(
            [jnp.where(odd, vy, vx), jnp.where(odd, vx, vy), jnp.where(odd, b, vz), jnp.where(odd, vz, b)], axis=0
        )
        high, low = halves(data)
        nt = ((1,), (1,))
        value = dot(zf[0], high, nt) + dot(zf[1], high, nt) + dot(zf[0], low, nt)
        for g in range(2):
            send1[g, pl.ds(a, MZ, stride=XL), :] = value[:, g * 128 : (g + 1) * 128]

    pl.semaphore_wait(barrier, W + 6)

    def wide_send(src, dst, chunk, ssem, rsem):
        @pl.loop(0, W)
        def _(k):
            peer = wide_peer(k)
            pltpu.make_async_remote_copy(
                src_ref=src.at[:, rows((chunk * W + peer) * XL, XL), :],
                dst_ref=dst.at[:, rows((chunk * W + w) * XL, XL), :],
                send_sem=ssem.at[chunk],
                recv_sem=rsem.at[chunk],
                device_id=(peer, across),
                device_id_type=MESH,
            ).start()

    def narrow_send(src, dst, chunk, ssem, rsem, source_slot, target_slot):
        @pl.loop(1, N)
        def _(k):
            peer = narrow_peer(k)
            pltpu.make_async_remote_copy(
                src_ref=src.at[:, rows((chunk * N + source_slot(peer)) * PL, PL), :],
                dst_ref=dst.at[:, rows((chunk * N + target_slot) * PL, PL), :],
                send_sem=ssem.at[chunk],
                recv_sem=rsem.at[chunk],
                device_id=(w, peer),
                device_id_type=MESH,
            ).start()

        pltpu.make_async_copy(
            src.at[:, rows((chunk * N + source_slot(n)) * PL, PL), :],
            dst.at[:, rows((chunk * N + target_slot) * PL, PL), :],
            rsem.at[chunk],
        ).start()

    def wait(buffer, chunk, size, sem, part=None):
        ref = buffer.at[:, rows(chunk * size, part or size), :]
        pltpu.make_async_copy(ref, ref, sem.at[chunk]).wait()

    @pl.loop(0, QL)
    def _(chunk):
        wide_send(send1, recv1, chunk, s1, r1)

    low_lanes = lax.broadcasted_iota(jnp.int32, (PL, 128), 1) < 64

    def x_step(chunk):
        wait(recv1, chunk, NX, r1)
        for g in range(2):
            high, low = halves(recv1[g, rows(chunk * NX, NX), :])
            xh[:, g * 128 : (g + 1) * 128] = high
            xl[:, g * 128 : (g + 1) * 128] = low

        @pl.loop(0, MX // 256)
        def _(m):
            part = rows(m * 256, 256)
            value = dot3(xf[0, part, :], xf[1, part, :], xh[...], xl[...])
            for g in range(2):
                send2[g, rows(chunk * MX + m * 256, 256), :] = value[:, g * 128 : (g + 1) * 128]

        narrow_send(send2, recv2, chunk, s2, r2, lambda peer: peer, across)

    def y_step(t):
        for q in range(2):
            chunk = 2 * t + q
            wait(recv2, chunk, MX, r2)
            for g in range(2):
                for s in range(4):
                    first = recv2[g, rows(chunk * MX + 2 * s * PL, PL), :]
                    second = recv2[g, rows(chunk * MX + (2 * s + 1) * PL, PL), :]
                    even = jnp.where(low_lanes, first, second)
                    other = pltpu.roll(jnp.where(low_lanes, second, first), 64, 1)
                    for f, value in ((2 * g, even), (2 * g + 1, other)):
                        high, low = halves(value)
                        place = pl.ds((q * 4 + f) * PL, PL)
                        yh[place, s * 128 : (s + 1) * 128] = high
                        yl[place, s * 128 : (s + 1) * 128] = low
        for q in range(2):
            part = pl.ds(q * 4 * PL, 4 * PL)
            for j in range(MY // 256):
                cols = pl.ds(j * 256, 256)
                grid = dot3(yh[part, :], yl[part, :], yf[0, :, cols], yf[1, :, cols])
                for f, place in ((0, 0), (2, 1), (1, 2)):
                    flux = grid[f * PL : (f + 1) * PL] * grid[3 * PL :]
                    high, low = halves(flux)
                    gh[pl.ds((place * 2 + q) * PL, PL), cols] = high
                    gl[pl.ds((place * 2 + q) * PL, PL), cols] = low
        for table, start, fields in ((yb, 0, (0, 2)), (ys, 4 * PL, (1,))):
            part = pl.ds(start, 2 * PL * len(fields))
            for j in range(NY // 256):
                cols = pl.ds(j * 256, 256)
                value = dot3(gh[part, :], gl[part, :], table[0, :, cols], table[1, :, cols])
                for i, f in enumerate(fields):
                    for h in range(2):
                        lanes = slice(h * 128, (h + 1) * 128)
                        first = value[2 * i * PL : (2 * i + 1) * PL, lanes]
                        second = pltpu.roll(value[(2 * i + 1) * PL : (2 * i + 2) * PL, lanes], 64, 1)
                        block = (2 * j + h) * 2
                        send3[f, rows((t * N + block) * PL, PL), :] = jnp.where(low_lanes, first, second)
                        send3[f, rows((t * N + block + 1) * PL, PL), :] = jnp.where(low_lanes, second, first)
        narrow_send(send3, recv3, t, s3, r3, lambda peer: lax.rem(peer + 4, N), n)

    def x_back_step(t):
        wait(recv3, t, MX, r3)
        for f in range(3):
            high, low = halves(recv3[f, rows(t * MX, MX), :])
            bh[:, f * 128 : (f + 1) * 128] = high
            bl[:, f * 128 : (f + 1) * 128] = low

        @pl.loop(0, NX // 256)
        def _(m):
            part = rows(m * 256, 256)
            plain = dot3(xb[0, part, :], xb[1, part, :], bh[:, 128:], bl[:, 128:])
            sloped = dot3(xs[0, part, :], xs[1, part, :], bh[:, :128], bl[:, :128])
            send4[0, rows(t * NX + m * 256, 256), :] = plain[:, :128] + sloped
            send4[1, rows(t * NX + m * 256, 256), :] = plain[:, 128:]

        wide_send(send4, recv4, t, s4, r4)

    for copy in table_copies:
        copy.wait()

    @pl.loop(0, QL + 3)
    def _(i):
        pl.when(i < QL)(lambda: x_step(i))
        even = lax.rem(i, 2) == 0
        pl.when(even & (i >= 4))(lambda: x_back_step(i // 2 - 2))
        pl.when(even & (i >= 2) & (i < QL + 2))(lambda: y_step(i // 2 - 1))

    zh[...] = jnp.zeros_like(zh)
    zl[...] = jnp.zeros_like(zl)
    for t in range(PAIRS):
        wait(recv4, t, NX, r4)
    wide_lanes = lax.broadcasted_iota(jnp.int32, (NZ, 128), 1) < 64

    @pl.loop(0, XL // 2)
    def _(i):
        for side in range(2):
            for g in range(2):
                high, low = halves(recv4[g, pl.ds(2 * i + side, PAIRS * W, stride=XL), :])
                place = pl.ds(g * PAIRS * W, PAIRS * W)
                zh[place, side * 128 : (side + 1) * 128] = high
                zl[place, side * 128 : (side + 1) * 128] = low
        value = dot3(zb[0, parity], zb[1, parity], zh[...], zl[...])
        first = value[:NZ, :128] + pltpu.roll(value[NZ:, :128], 64, 1)
        second = pltpu.roll(value[:NZ, 128:], 64, 1) + value[NZ:, 128:]
        nonlinear = jnp.where(wide_lanes, first, second).T
        for side in range(2):
            buoyancy = b_ref[2 * i + side]
            right_side = buoyancy - (4.0 / NX) * nonlinear[side * YL : (side + 1) * YL]
            out_ref[2 * i + side] = right_side.astype(BF16)

    for c in range(QL):
        wait(send1, c, NX, s1)
        wait(send2, c, MX, s2, MX - PL)
    for t in range(PAIRS):
        wait(send3, t, MX, s3, MX - PL)
        wait(send4, t, NX, s4)


def right_side_of(buoyancy, velocity_x, velocity_y, velocity_z):
    zf, xf, yf, yb, ys, xb, xs, zb = [jnp.asarray(t) for t in tables()]
    vmem = pl.BlockSpec(memory_space=pltpu.VMEM)
    hbm = pl.BlockSpec(memory_space=pl.ANY)
    buffers = []
    for groups, count in ((2, QL * NX), (2, QL * MX), (3, PAIRS * MX), (2, PAIRS * NX)):
        buffers += [pltpu.VMEM((groups, count, 128), F32)] * 2
    split = []
    for shape in ((NX, 256), (8 * PL, NY), (6 * PL, MY), (MX, 384), (256, 256)):
        split += [pltpu.VMEM(shape, BF16)] * 2
    sems = [pltpu.SemaphoreType.DMA((count,)) for count in (6, QL, QL, QL, QL, PAIRS, PAIRS, PAIRS, PAIRS)]
    return pl.pallas_call(
        kernel,
        out_shape=jax.ShapeDtypeStruct((XL, YL, NZ), BF16),
        in_specs=[vmem] * 6 + [hbm] * 6,
        out_specs=vmem,
        scratch_shapes=buffers + [pltpu.VMEM(t.shape, BF16) for t in (xf, yf, yb, ys, xb, xs)] + split + sems,
        compiler_params=pltpu.CompilerParams(
            collective_id=1, has_side_effects=True, vmem_limit_bytes=60 * 1024 * 1024
        ),
        name="spectral",
    )(velocity_x, velocity_y, velocity_z, buoyancy, zf, zb, xf, yf, yb, ys, xb, xs)


def per_device(buoyancy, velocity_x, velocity_y, velocity_z, inverse_blocks):
    right_side = right_side_of(buoyancy, velocity_x, velocity_y, velocity_z)
    grouped = right_side.reshape(XL // 2, 2, YL // 2, 2, NZ)
    solved = jnp.einsum(
        "xyin,xaybn->xaybi", inverse_blocks, grouped, preferred_element_type=F32
    )
    return solved.reshape(XL, YL, NZ)


def solution(mesh):
    fields = P("wide", "narrow", None)
    return jax.shard_map(
        per_device,
        mesh=mesh,
        in_specs=(fields, fields, fields, fields, P("wide", "narrow", None, None)),
        out_specs=fields,
        check_vma=False,
    )
```

time: 663 us -> 195 us (0.29); the launches traced: 653 us -> 195 us
  waiting for transfers between devices: 264 us -> 0 us
  matrix products: 239 us -> 7.89 us
  Pallas kernels: 0 us -> 186 us
  local copies, waits for them, and re-layouts: 109 us -> 1.04 us
  starting transfers between devices: 36.4 us -> 0 us
    all_to_all x4 -> x0, waiting for transfers between devices: 264 us -> none  [the longest x1 105 us: per_device(): lax.all_to_all(along_y, 'wide', split_axis=2, concat_axis=1, tiled=True)]
    dot_general x7 -> x0, matrix products: 235 us -> none  [the longest x1 141 us: per_device(): grid = jnp.einsum('fsjqa,sap->fjqp', split, table, precision=HIGHEST)]
    pallas_call x0 -> x1, Pallas kernels: none -> 186 us  [right_side_of(): pl.pallas_call(kernel, out_shape=jax.ShapeDtypeStruct((XL, YL, NZ), BF16)...]
    reshape x8 -> x0, local copies, waits for them, and re-layouts: 79.9 us -> none  [the longest x2 31.1 us: per_device(): split = incoming.reshape(items, x_local, wide_count, q_part, j_part)]
    all_to_all x4 -> x0, starting transfers between devices: 36.4 us -> none  [the longest x1 11.9 us: per_device(): lax.all_to_all(along_y, 'wide', split_axis=2, concat_axis=1, tiled=True)]
    all_to_all x5 -> x0, local copies, waits for them, and re-layouts: 19.8 us -> none  [the longest x1 6.72 us: per_device(): lax.all_to_all(along_y, 'wide', split_axis=2, concat_axis=1, tiled=True)]
  transfers between devices with their start and end apart: 4 -> 0, of which waited for: 4 -> 0; matrix products, arithmetic and copies ran while one was open for 0% -> 0% of each run, Pallas kernels for 0% -> 0%
where the time goes in v1:
time: 195 us
  Pallas kernels  186 us (95%)
  matrix products  7.89 us (4%)
    pallas_call x1, Pallas kernels, right_side_of(): pl.pallas_call(kernel, out_shape=jax.ShapeDtypeStruct((XL, YL, NZ), BF16)...  186 us
    dot_general x1, matrix products, per_device(): jnp.einsum('xyin,xaybn->xaybi', inverse_blocks, grouped, preferred_elemen...  7.89 us

profile of v1, /device:TPU:1, one launch (start us, length us, event | category | flops | bytes accessed | tf_op | source)
XLA Modules:
  0.0 194.5 jit_solution(5415173977993645394)
XLA Ops:
  0.0 185.6 %spectral.1 = bf16[16,64,128]{2,1,0:T(8,128)(2,1)} custom-call(f32[16,64,128]{2,1,0:T(8,128)} %vx_ref.1, f32[16,64,128]{2,1,0:T(8,128)} %vy_ref.1, f32[16,64,128]{2,1,0:T(8,128)} %vz_ref.1, f32[16,64,128]{2,1,0:T(8,128)} %b_ref.1, bf16[2,192,128]{2,1,0:T(8,128)(2,1)} %constant.16.clone.zf, bf16[2,2,256,256]{3,2,1,0:T(8,128)(2,1)} %constant.23.clone.zb, ...), custom_call_target="tpu_custom_call" | custom-call | tf_op jit(solution)/shard_map/spectral/pallas_call | solution.py:345
  185.6 7.9 %fusion.2 = f32[8,2,32,2,128]{4,3,1,2,0:T(2,128)S(1)} fusion(bf16[8,32,128,128]{3,2,1,0:T(8,128)(2,1)} %param.17, bf16[8,2,32,2,128]{4,3,2,1,0:T(2,128)(2,1)} %bitcast.11), kind=kOutput, calls=%fused_computation.2 | convolution fusion | flops 33554432 | bytes 9175040 | tf_op jit(solution)/shard_map/xyin,xaybn->xaybi/dot_general | solution.py:361
  193.5 1.0 copy.16

commit v2 on v1

v2 whole, which is shorter than its diff:
```python
import functools

import jax
import jax.numpy as jnp
import ml_dtypes
import numpy as np
from jax import lax
from jax.experimental import pallas as pl
from jax.experimental.pallas import tpu as pltpu
from jax.sharding import PartitionSpec as P

NX = 512
NY = 512
NZ = 128
MX = 768
MY = 768
MZ = 192
W = 32
N = 8
XL = NX // W
YL = NY // N
QL = MZ // W
PL = MX // N
HALF = PL // 2
F32 = jnp.float32
BF16 = jnp.bfloat16
MESH = pl.DeviceIdType.MESH


def fourier_table(n_coef, n_grid):
    index = np.arange(n_coef)
    phase = (index[:, None] // 2 * np.arange(n_grid)[None, :] % n_grid) * (2.0 * np.pi / n_grid)
    return np.where((index % 2 == 0)[:, None], np.cos(phase), np.sin(phase))


def fourier_inverse(n_coef, n_grid):
    index = np.arange(n_coef)
    modes = index // 2
    weight = np.where(modes == 0, np.where(index % 2 == 0, 1.0 / n_grid, 0.0), 2.0 / n_grid)
    return fourier_table(n_coef, n_grid).T * weight[None, :]


def cheb_table(n_coef, n_grid):
    orders = np.arange(n_coef)
    points = np.arange(n_grid)
    index_grid = orders[:, None] * (2 * points[None, :] + 1) % (4 * n_grid)
    return np.cos(index_grid * (np.pi / (2 * n_grid)))


def cheb_inverse(n_coef, n_grid):
    weight = np.where(np.arange(n_coef) == 0, 1.0 / n_grid, 2.0 / n_grid)
    return cheb_table(n_coef, n_grid).T * weight[None, :]


def cheb_slope(n_coef):
    rows = np.arange(n_coef)[:, None]
    cols = np.arange(n_coef)[None, :]
    inside = (cols > rows) & ((cols - rows) % 2 == 1)
    return np.where(inside, np.where(rows == 0, 1.0, 2.0) * cols, 0.0)


def split_table(table):
    high = table.astype(np.float32).astype(ml_dtypes.bfloat16)
    low = (table - high.astype(np.float64)).astype(np.float32).astype(ml_dtypes.bfloat16)
    return np.stack([high, low])


@functools.cache
def tables():
    z_forward = cheb_table(NZ, MZ).T.reshape(W, QL, NZ).transpose(1, 0, 2).reshape(MZ, NZ)
    x_forward = fourier_table(NX, MX).T
    y_forward = fourier_table(NY, MY)
    y_backward = fourier_inverse(NY, MY)
    x_backward = fourier_inverse(NX, MX).T
    plain = cheb_inverse(NZ, MZ)
    z_backward = np.zeros((2, NZ, 256))
    for i, source in enumerate((plain, plain @ cheb_slope(NZ).T)):
        z_backward[i, :, :MZ] = source.reshape(W, QL, NZ).transpose(2, 1, 0).reshape(NZ, MZ)
    z_backward = z_backward.reshape(2 * NZ, 256)
    return [split_table(t) for t in (z_forward, x_forward, y_forward, y_backward, x_backward, z_backward)]


def halves(value):
    high = value.astype(BF16)
    return high, (value - high.astype(F32)).astype(BF16)


def dot(a, b, dims=((1,), (0,))):
    return lax.dot_general(a, b, (dims, ((), ())), preferred_element_type=F32)


def dot3(a_high, a_low, b_high, b_low):
    return dot(a_high, b_high) + dot(a_low, b_high) + dot(a_high, b_low)


def rows(start, size):
    return pl.ds(pl.multiple_of(start, 16), size)


def kernel(
    vx_ref, vy_ref, vz_ref, b_ref, zf, zb, xf_hbm, yf_hbm, yb_hbm, xb_hbm,
    out_ref,
    send1, recv1, send2, recv2, send3, recv3, send4, recv4,
    xf, yf, yb, xb,
    xh, xl, yh, yl, gh, gl, bh, bl, zh, zl,
    table_sem, s1, r1, s2, r2, s3, r3, s4, r4,
):
    w = lax.axis_index("wide")
    n = lax.axis_index("narrow")
    across = lax.rem(n + 4, N)
    parity = lax.rem(n, 2)
    z_pos, rest = w // 4, lax.rem(w, 4)
    y_pos, x_pos = n // 4, lax.rem(n, 4)

    def wide_peer(k):
        step, turn = lax.rem(k, 8), k // 8
        hops = step // 2 + 1
        shift = jnp.where(step == 7, 0, jnp.where(lax.rem(step, 2) == 0, hops, 8 - hops))
        return lax.rem(z_pos + shift, 8) * 4 + lax.rem(rest + turn, 4)

    def narrow_peer(k):
        y_shift = jnp.where(k < 3, lax.rem(k, 3) // 2, jnp.where(k == 5, 0, 1))
        x_shift = jnp.where(
            k < 2, 1 + 2 * k, jnp.where(k == 2, 0, jnp.where(k < 5, 2 * k - 5, 2))
        )
        return lax.rem(y_pos + y_shift, 2) * 4 + lax.rem(x_pos + x_shift, 4)

    def flipped(wide):
        return wide + 2 - 4 * lax.rem(wide // 2, 2)

    def flips(wide, chunk):
        return lax.rem(wide + chunk, 2) == 1

    def plane(chunk):
        return jnp.where(flips(w, chunk) & (y_pos == 0), flipped(w), w)

    table_copies = [
        pltpu.make_async_copy(hbm, vmem, table_sem.at[i])
        for i, (hbm, vmem) in enumerate(
            ((xf_hbm, xf), (yf_hbm, yf), (yb_hbm, yb), (xb_hbm, xb))
        )
    ]
    for copy in table_copies:
        copy.start()

    barrier = pltpu.get_barrier_semaphore()

    @pl.loop(0, W)
    def _(k):
        pl.semaphore_signal(barrier, inc=1, device_id=(wide_peer(k), across), device_id_type=MESH)

    for k in (0, 1, 3, 4, 5, 6):
        pl.semaphore_signal(barrier, inc=1, device_id=(w, narrow_peer(k)), device_id_type=MESH)
    for k in (3, 4, 6):
        pl.semaphore_signal(barrier, inc=1, device_id=(flipped(w), narrow_peer(k)), device_id_type=MESH)

    odd = parity == 1

    @pl.loop(0, XL)
    def _(a):
        vx, vy, vz, b = vx_ref[a], vy_ref[a], vz_ref[a], b_ref[a]
        data = jnp.concatenate(
            [jnp.where(odd, vy, vx), jnp.where(odd, vx, vy), jnp.where(odd, b, vz), jnp.where(odd, vz, b)], axis=0
        )
        high, low = halves(data)
        nt = ((1,), (1,))
        value = dot(zf[0], high, nt) + dot(zf[1], high, nt) + dot(zf[0], low, nt)
        for g in range(2):
            send1[g, pl.ds(a, MZ, stride=XL), :] = value[:, g * 128 : (g + 1) * 128]

    pl.semaphore_wait(barrier, W + 9)

    def wide_send(src, dst, chunk, ssem, rsem, target, slot):
        @pl.loop(0, W)
        def _(k):
            peer = wide_peer(k)
            pltpu.make_async_remote_copy(
                src_ref=src.at[:, rows((chunk * W + peer) * XL, XL), :],
                dst_ref=dst.at[:, rows((chunk * W + slot) * XL, XL), :],
                send_sem=ssem.at[chunk],
                recv_sem=rsem.at[chunk],
                device_id=(target(peer), across),
                device_id_type=MESH,
            ).start()

    def narrow_send(src, dst, chunk, size, ssem, rsem, source_slot, target_slot):
        def block(slot):
            return rows((chunk * N + slot) * size, size)

        @pl.loop(0, N - 1)
        def _(k):
            peer = narrow_peer(k)
            wide = jnp.where(flips(w, chunk) & (peer // 4 != y_pos), flipped(w), w)
            pltpu.make_async_remote_copy(
                src_ref=src.at[:, block(source_slot(peer)), :],
                dst_ref=dst.at[:, block(target_slot), :],
                send_sem=ssem.at[chunk],
                recv_sem=rsem.at[chunk],
                device_id=(wide, peer),
                device_id_type=MESH,
            ).start()

        pltpu.make_async_copy(
            src.at[:, block(source_slot(n)), :], dst.at[:, block(target_slot), :], rsem.at[chunk]
        ).start()

    def wait(buffer, chunk, size, sem, part=None):
        ref = buffer.at[:, rows(chunk * size, part or size), :]
        pltpu.make_async_copy(ref, ref, sem.at[chunk]).wait()

    @pl.loop(0, QL)
    def _(chunk):
        def holder(peer):
            return jnp.where(flips(peer, chunk) & (y_pos == 1), flipped(peer), peer)

        wide_send(send1, recv1, chunk, s1, r1, holder, w)

    low_lanes = lax.broadcasted_iota(jnp.int32, (PL, 128), 1) < 64
    half_lanes = lax.broadcasted_iota(jnp.int32, (HALF, 128), 1) < 64

    def x_step(chunk):
        wait(recv1, chunk, NX, r1)
        for g in range(2):
            high, low = halves(recv1[g, rows(chunk * NX, NX), :])
            xh[:, g * 128 : (g + 1) * 128] = high
            xl[:, g * 128 : (g + 1) * 128] = low

        @pl.loop(0, MX // 256)
        def _(m):
            part = rows(m * 256, 256)
            value = dot3(xf[0, part, :], xf[1, part, :], xh[...], xl[...])
            for g in range(2):
                send2[g, rows(chunk * MX + m * 256, 256), :] = value[:, g * 128 : (g + 1) * 128]

        narrow_send(send2, recv2, chunk, PL, s2, r2, lambda peer: peer, across)

    def y_step(chunk):
        wait(recv2, chunk, MX, r2)
        for g in range(2):
            for s in range(4):
                first = recv2[g, rows(chunk * MX + 2 * s * PL, PL), :]
                second = recv2[g, rows(chunk * MX + (2 * s + 1) * PL, PL), :]
                even = jnp.where(low_lanes, first, second)
                other = pltpu.roll(jnp.where(low_lanes, second, first), 64, 1)
                for f, value in ((2 * g, even), (2 * g + 1, other)):
                    high, low = halves(value)
                    yh[f * PL : (f + 1) * PL, s * 128 : (s + 1) * 128] = high
                    yl[f * PL : (f + 1) * PL, s * 128 : (s + 1) * 128] = low
        for j in range(MY // 256):
            cols = pl.ds(j * 256, 256)
            grid = dot3(yh[...], yl[...], yf[0, :, cols], yf[1, :, cols])
            for f in range(3):
                high, low = halves(grid[f * PL : (f + 1) * PL] * grid[3 * PL :])
                gh[f * PL : (f + 1) * PL, cols] = high
                gl[f * PL : (f + 1) * PL, cols] = low
        lane = lax.broadcasted_iota(jnp.int32, (PL, 128), 1)
        for j in range(NY // 256):
            cols = pl.ds(j * 256, 256)
            value = dot3(gh[...], gl[...], yb[0, :, cols], yb[1, :, cols])
            for f in range(3):
                for h in range(2):
                    part = value[f * PL : (f + 1) * PL, h * 128 : (h + 1) * 128]
                    if f == 1:
                        mode = (lane // 2 + (2 * j + h) * 64).astype(F32)
                        part = jnp.where(
                            lane % 2 == 0, mode * pltpu.roll(part, 127, 1), -mode * pltpu.roll(part, 1, 1)
                        )
                    first, second = part[:HALF], pltpu.roll(part[HALF:], 64, 1)
                    block = chunk * N + (2 * j + h) * 2
                    send3[f, rows(block * HALF, HALF), :] = jnp.where(half_lanes, first, second)
                    send3[f, rows((block + 1) * HALF, HALF), :] = jnp.where(half_lanes, second, first)
        narrow_send(send3, recv3, chunk, HALF, s3, r3, lambda peer: lax.rem(peer + 4, N), n)

    def x_back_step(chunk):
        wait(recv3, chunk, N * HALF, r3)
        for s in range(N):
            flux_x, flux_y, flux_z = (recv3[f, rows((chunk * N + s) * HALF, HALF), :] for f in range(3))
            near = jnp.where(half_lanes, flux_y, pltpu.roll(flux_z, 64, 1))
            far = jnp.where(half_lanes, pltpu.roll(flux_y, 64, 1), flux_z)
            for side, yz, x in ((parity, near, flux_x), (1 - parity, far, pltpu.roll(flux_x, 64, 1))):
                place = rows(s * PL + side * HALF, HALF)
                for lanes, value in ((slice(0, 128), yz), (slice(128, 256), x)):
                    high, low = halves(value)
                    bh[place, lanes] = high
                    bl[place, lanes] = low

        row = lax.broadcasted_iota(jnp.int32, (256, 128), 0)
        lane = lax.broadcasted_iota(jnp.int32, (256, 128), 1)
        for m in range(NX // 256):
            part = pl.ds(m * 256, 256)
            value = dot3(xb[0, part, :], xb[1, part, :], bh[...], bl[...])
            x = value[:, 128:]
            mode = (row // 2 + m * 128).astype(F32)
            sloped = jnp.where(row % 2 == 0, mode * pltpu.roll(x, 255, 0), -mode * pltpu.roll(x, 1, 0))
            send4[0, rows(chunk * NX + m * 256, 256), :] = value[:, :128] + jnp.where(lane < 64, sloped, 0.0)

        wide_send(send4, recv4, chunk, s4, r4, lambda peer: peer, plane(chunk))

    for copy in table_copies:
        copy.wait()

    @pl.loop(0, QL + 2)
    def _(i):
        pl.when(i < QL)(lambda: x_step(i))
        pl.when((i >= 1) & (i < QL + 1))(lambda: y_step(i - 1))
        pl.when(i >= 2)(lambda: x_back_step(i - 2))

    zh[...] = jnp.zeros_like(zh)
    zl[...] = jnp.zeros_like(zl)
    for c in range(QL):
        wait(recv4, c, NX, r4)
    wide_lanes = lax.broadcasted_iota(jnp.int32, (NZ, 128), 1) < 64

    @pl.loop(0, XL // 2)
    def _(i):
        for side in range(2):
            high, low = halves(recv4[0, pl.ds(2 * i + side, MZ, stride=XL), :])
            zh[:MZ, side * 128 : (side + 1) * 128] = high
            zl[:MZ, side * 128 : (side + 1) * 128] = low
        value = dot3(zb[0], zb[1], zh[...], zl[...])
        first = value[:NZ, :128] + pltpu.roll(value[NZ:, :128], 64, 1)
        second = pltpu.roll(value[:NZ, 128:], 64, 1) + value[NZ:, 128:]
        nonlinear = jnp.where(wide_lanes, first, second).T
        for side in range(2):
            buoyancy = b_ref[2 * i + side]
            right_side = buoyancy - (4.0 / NX) * nonlinear[side * YL : (side + 1) * YL]
            out_ref[2 * i + side] = right_side.astype(BF16)

    for c in range(QL):
        wait(send1, c, NX, s1)
        wait(send2, c, MX, s2, MX - PL)
        wait(send3, c, N * HALF, s3, (N - 1) * HALF)
        wait(send4, c, NX, s4)


def right_side_of(buoyancy, velocity_x, velocity_y, velocity_z):
    zf, xf, yf, yb, xb, zb = [jnp.asarray(t) for t in tables()]
    vmem = pl.BlockSpec(memory_space=pltpu.VMEM)
    hbm = pl.BlockSpec(memory_space=pl.ANY)
    buffers = []
    for groups, count in ((2, QL * NX), (2, QL * MX), (3, QL * N * HALF), (1, QL * NX)):
        buffers += [pltpu.VMEM((groups, count, 128), F32)] * 2
    split = []
    for shape in ((NX, 256), (4 * PL, NY), (3 * PL, MY), (MX, 256), (256, 256)):
        split += [pltpu.VMEM(shape, BF16)] * 2
    sems = [pltpu.SemaphoreType.DMA((count,)) for count in (4,) + (QL,) * 8]
    return pl.pallas_call(
        kernel,
        out_shape=jax.ShapeDtypeStruct((XL, YL, NZ), BF16),
        in_specs=[vmem] * 6 + [hbm] * 4,
        out_specs=vmem,
        scratch_shapes=buffers + [pltpu.VMEM(t.shape, BF16) for t in (xf, yf, yb, xb)] + split + sems,
        compiler_params=pltpu.CompilerParams(
            collective_id=1, has_side_effects=True, vmem_limit_bytes=60 * 1024 * 1024
        ),
        name="spectral",
    )(velocity_x, velocity_y, velocity_z, buoyancy, zf, zb, xf, yf, yb, xb)


def per_device(buoyancy, velocity_x, velocity_y, velocity_z, inverse_blocks):
    right_side = right_side_of(buoyancy, velocity_x, velocity_y, velocity_z)
    grouped = right_side.reshape(XL // 2, 2, YL // 2, 2, NZ)
    solved = jnp.einsum(
        "xyin,xaybn->xaybi", inverse_blocks, grouped, preferred_element_type=F32
    )
    return solved.reshape(XL, YL, NZ)


def solution(mesh):
    fields = P("wide", "narrow", None)
    return jax.shard_map(
        per_device,
        mesh=mesh,
        in_specs=(fields, fields, fields, fields, P("wide", "narrow", None, None)),
        out_specs=fields,
        check_vma=False,
    )
```

time: 195 us -> 150 us (0.77)
  Pallas kernels: 186 us -> 141 us
    pallas_call x1, Pallas kernels: 186 us -> 141 us  [right_side_of(): pl.pallas_call(kernel, out_shape=jax.ShapeDtypeStruct((XL, YL, NZ), BF16)...]
where the time goes in v2:
time: 150 us
  Pallas kernels  141 us (94%)
  matrix products  7.89 us (5%)
    pallas_call x1, Pallas kernels, right_side_of(): pl.pallas_call(kernel, out_shape=jax.ShapeDtypeStruct((XL, YL, NZ), BF16)...  141 us
    dot_general x1, matrix products, per_device(): jnp.einsum('xyin,xaybn->xaybi', inverse_blocks, grouped, preferred_elemen...  7.89 us

profile of v2, /device:TPU:1, one launch (start us, length us, event | category | flops | bytes accessed | tf_op | source)
XLA Modules:
  0.0 150.1 jit_solution(13242634968651890308)
XLA Ops:
  0.0 141.1 %spectral.1 = bf16[16,64,128]{2,1,0:T(8,128)(2,1)} custom-call(f32[16,64,128]{2,1,0:T(8,128)} %vx_ref.1, f32[16,64,128]{2,1,0:T(8,128)} %vy_ref.1, f32[16,64,128]{2,1,0:T(8,128)} %vz_ref.1, f32[16,64,128]{2,1,0:T(8,128)} %b_ref.1, bf16[2,192,128]{2,1,0:T(8,128)(2,1)} %constant.12.clone.zf, bf16[2,256,256]{2,1,0:T(8,128)(2,1)} %constant.17.clone.zb, ...), custom_call_target="tpu_custom_call" | custom-call | tf_op jit(solution)/shard_map/spectral/pallas_call | solution.py:347
  141.1 7.9 %fusion.2 = f32[8,2,32,2,128]{4,3,1,2,0:T(2,128)S(1)} fusion(bf16[8,32,128,128]{3,2,1,0:T(8,128)(2,1)} %param.15, bf16[8,2,32,2,128]{4,3,2,1,0:T(2,128)(2,1)} %bitcast.11), kind=kOutput, calls=%fused_computation.2 | convolution fusion | flops 33554432 | bytes 9175040 | tf_op jit(solution)/shard_map/xyin,xaybn->xaybi/dot_general | solution.py:363
  149.0 1.0 copy.14

commit v3 on v2

--- a/solution.py
+++ b/solution.py
@@ -98,10 +98,10 @@
 
 
 def kernel(
-    vx_ref, vy_ref, vz_ref, b_ref, zf, zb, xf_hbm, yf_hbm, yb_hbm, xb_hbm,
+    vx_hbm, vy_hbm, vz_hbm, b_hbm, zf_hbm, zb_hbm, xf_hbm, yf_hbm, yb_hbm, xb_hbm,
     out_ref,
     send1, recv1, send2, recv2, send3, recv3, send4, recv4,
-    xf, yf, yb, xb,
+    vx_ref, vy_ref, vz_ref, b_ref, zf, zb, xf, yf, yb, xb,
     xh, xl, yh, yl, gh, gl, bh, bl, zh, zl,
     table_sem, s1, r1, s2, r2, s3, r3, s4, r4,
 ):
@@ -137,7 +137,10 @@
     table_copies = [
         pltpu.make_async_copy(hbm, vmem, table_sem.at[i])
         for i, (hbm, vmem) in enumerate(
-            ((xf_hbm, xf), (yf_hbm, yf), (yb_hbm, yb), (xb_hbm, xb))
+            (
+                (vx_hbm, vx_ref), (vy_hbm, vy_ref), (vz_hbm, vz_ref), (b_hbm, b_ref), (zf_hbm, zf),
+                (xf_hbm, xf), (yf_hbm, yf), (yb_hbm, yb), (xb_hbm, xb), (zb_hbm, zb),
+            )
         )
     ]
     for copy in table_copies:
@@ -154,19 +157,25 @@
     for k in (3, 4, 6):
         pl.semaphore_signal(barrier, inc=1, device_id=(flipped(w), narrow_peer(k)), device_id_type=MESH)
 
+    for copy in table_copies[:5]:
+        copy.wait()
     odd = parity == 1
 
-    @pl.loop(0, XL)
-    def _(a):
+    def z_step(a, part, size):
         vx, vy, vz, b = vx_ref[a], vy_ref[a], vz_ref[a], b_ref[a]
         data = jnp.concatenate(
             [jnp.where(odd, vy, vx), jnp.where(odd, vx, vy), jnp.where(odd, b, vz), jnp.where(odd, vz, b)], axis=0
         )
         high, low = halves(data)
         nt = ((1,), (1,))
-        value = dot(zf[0], high, nt) + dot(zf[1], high, nt) + dot(zf[0], low, nt)
+        first, second = zf[0, part : part + size], zf[1, part : part + size]
+        value = dot(first, high, nt) + dot(second, high, nt) + dot(first, low, nt)
         for g in range(2):
-            send1[g, pl.ds(a, MZ, stride=XL), :] = value[:, g * 128 : (g + 1) * 128]
+            send1[g, pl.ds(part * XL + a, size, stride=XL), :] = value[:, g * 128 : (g + 1) * 128]
+
+    @pl.loop(0, XL)
+    def _(a):
+        z_step(a, 0, W)
 
     pl.semaphore_wait(barrier, W + 9)
 
@@ -208,12 +217,21 @@
         ref = buffer.at[:, rows(chunk * size, part or size), :]
         pltpu.make_async_copy(ref, ref, sem.at[chunk]).wait()
 
-    @pl.loop(0, QL)
-    def _(chunk):
+    def forward(chunk):
         def holder(peer):
             return jnp.where(flips(peer, chunk) & (y_pos == 1), flipped(peer), peer)
 
         wide_send(send1, recv1, chunk, s1, r1, holder, w)
+
+    forward(0)
+
+    @pl.loop(0, XL)
+    def _(a):
+        z_step(a, W, MZ - W)
+
+    @pl.loop(1, QL)
+    def _(chunk):
+        forward(chunk)
 
     low_lanes = lax.broadcasted_iota(jnp.int32, (PL, 128), 1) < 64
     half_lanes = lax.broadcasted_iota(jnp.int32, (HALF, 128), 1) < 64
@@ -296,7 +314,7 @@
 
         wide_send(send4, recv4, chunk, s4, r4, lambda peer: peer, plane(chunk))
 
-    for copy in table_copies:
+    for copy in table_copies[5:]:
         copy.wait()
 
     @pl.loop(0, QL + 2)
@@ -336,22 +354,23 @@
 def right_side_of(buoyancy, velocity_x, velocity_y, velocity_z):
     zf, xf, yf, yb, xb, zb = [jnp.asarray(t) for t in tables()]
     vmem = pl.BlockSpec(memory_space=pltpu.VMEM)
-    hbm = pl.BlockSpec(memory_space=pl.ANY)
+    hbm = pl.BlockSpec(memory_space=pltpu.HBM)
+    fields = [pltpu.VMEM((XL, YL, NZ), F32)] * 4
     buffers = []
     for groups, count in ((2, QL * NX), (2, QL * MX), (3, QL * N * HALF), (1, QL * NX)):
         buffers += [pltpu.VMEM((groups, count, 128), F32)] * 2
     split = []
     for shape in ((NX, 256), (4 * PL, NY), (3 * PL, MY), (MX, 256), (256, 256)):
         split += [pltpu.VMEM(shape, BF16)] * 2
-    sems = [pltpu.SemaphoreType.DMA((count,)) for count in (4,) + (QL,) * 8]
+    sems = [pltpu.SemaphoreType.DMA((count,)) for count in (10,) + (QL,) * 8]
     return pl.pallas_call(
         kernel,
         out_shape=jax.ShapeDtypeStruct((XL, YL, NZ), BF16),
-        in_specs=[vmem] * 6 + [hbm] * 4,
+        in_specs=[hbm] * 10,
         out_specs=vmem,
-        scratch_shapes=buffers + [pltpu.VMEM(t.shape, BF16) for t in (xf, yf, yb, xb)] + split + sems,
+        scratch_shapes=buffers + fields + [pltpu.VMEM(t.shape, BF16) for t in (zf, zb, xf, yf, yb, xb)] + split + sems,
         compiler_params=pltpu.CompilerParams(
-            collective_id=1, has_side_effects=True, vmem_limit_bytes=60 * 1024 * 1024
+            collective_id=1, has_side_effects=True, vmem_limit_bytes=55 * 1024 * 1024
         ),
         name="spectral",
     )(velocity_x, velocity_y, velocity_z, buoyancy, zf, zb, xf, yf, yb, xb)

time: 150 us -> 146 us (0.973)
  matrix products: 7.89 us -> 5.36 us
  Pallas kernels: 141 us -> 139 us
    dot_general x1, matrix products: 7.89 us -> 5.36 us  [per_device(): jnp.einsum('xyin,xaybn->xaybi', inverse_blocks, grouped, preferred_elemen...]
    pallas_call x1, Pallas kernels: 141 us -> 139 us  [right_side_of(): pl.pallas_call(kernel, out_shape=jax.ShapeDtypeStruct((XL, YL, NZ), BF16)...]
where the time goes in v3:
time: 146 us
  Pallas kernels  139 us (95%)
  matrix products  5.36 us (4%)
    pallas_call x1, Pallas kernels, right_side_of(): pl.pallas_call(kernel, out_shape=jax.ShapeDtypeStruct((XL, YL, NZ), BF16)...  139 us
    dot_general x1, matrix products, per_device(): jnp.einsum('xyin,xaybn->xaybi', inverse_blocks, grouped, preferred_elemen...  5.36 us

profile of v3, /device:TPU:1, one launch (start us, length us, event | category | flops | bytes accessed | tf_op | source)
XLA Modules:
  0.0 145.8 jit_solution(13087572326620254803)
XLA Ops:
  0.0 0.0 copy-start
  0.0 139.4 %spectral.1 = bf16[16,64,128]{2,1,0:T(8,128)(2,1)} custom-call(f32[16,64,128]{2,1,0:T(8,128)} %vx_hbm.1, f32[16,64,128]{2,1,0:T(8,128)} %vy_hbm.1, f32[16,64,128]{2,1,0:T(8,128)} %vz_hbm.1, f32[16,64,128]{2,1,0:T(8,128)} %b_hbm.1, bf16[2,192,128]{2,1,0:T(8,128)(2,1)} %constant.12.clone.zf_hbm, bf16[2,256,256]{2,1,0:T(8,128)(2,1)} %constant.17.clone.zb_hbm, ...), custom_call_target="tpu_custom_call" | custom-call | tf_op jit(solution)/shard_map/spectral/pallas_call | solution.py:366
  139.4 0.0 copy-done
  139.4 5.4 %fusion.2 = f32[8,2,32,2,128]{4,3,1,2,0:T(2,128)S(1)} fusion(bf16[8,32,128,128]{3,2,1,0:T(8,128)(2,1)S(1)} %copy-done, bf16[8,2,32,2,128]{4,3,2,1,0:T(2,128)(2,1)} %bitcast.11), kind=kOutput, calls=%fused_computation.2 | convolution fusion | flops 33554432 | bytes 9175040 | tf_op jit(solution)/shard_map/xyin,xaybn->xaybi/dot_general | solution.py:382
  144.8 1.0 copy.14
Async XLA Ops:
  0.0 139.4 %copy-start = (bf16[8,32,128,128]{3,2,1,0:T(8,128)(2,1)S(1)}, bf16[8,32,128,128]{3,2,1,0:T(8,128)(2,1)}, u32[]{:S(2)}) copy-start(bf16[8,32,128,128]{3,2,1,0:T(8,128)(2,1)} %param.15) | copy-start | bytes 25165828

commit v4 on v3

--- a/solution.py
+++ b/solution.py
@@ -114,15 +114,13 @@
 
     def wide_peer(k):
         step, turn = lax.rem(k, 8), k // 8
-        hops = step // 2 + 1
-        shift = jnp.where(step == 7, 0, jnp.where(lax.rem(step, 2) == 0, hops, 8 - hops))
+        away = (step + 1) // 2
+        shift = jnp.where(lax.rem(step, 2) == 1, 4 - away, 4 + away)
         return lax.rem(z_pos + shift, 8) * 4 + lax.rem(rest + turn, 4)
 
     def narrow_peer(k):
-        y_shift = jnp.where(k < 3, lax.rem(k, 3) // 2, jnp.where(k == 5, 0, 1))
-        x_shift = jnp.where(
-            k < 2, 1 + 2 * k, jnp.where(k == 2, 0, jnp.where(k < 5, 2 * k - 5, 2))
-        )
+        y_shift = jnp.where((k == 0) | (k == 2) | (k == 3) | (k == 6), 1, 0)
+        x_shift = jnp.where(k < 2, 2, jnp.where(k == 6, 0, 1 + 2 * lax.rem(k, 2)))
         return lax.rem(y_pos + y_shift, 2) * 4 + lax.rem(x_pos + x_shift, 4)
 
     def flipped(wide):
@@ -152,9 +150,9 @@
     def _(k):
         pl.semaphore_signal(barrier, inc=1, device_id=(wide_peer(k), across), device_id_type=MESH)
 
-    for k in (0, 1, 3, 4, 5, 6):
+    for k in range(6):
         pl.semaphore_signal(barrier, inc=1, device_id=(w, narrow_peer(k)), device_id_type=MESH)
-    for k in (3, 4, 6):
+    for k in (0, 2, 3):
         pl.semaphore_signal(barrier, inc=1, device_id=(flipped(w), narrow_peer(k)), device_id_type=MESH)
 
     for copy in table_copies[:5]:

time: 146 us -> 144 us (0.986)
  Pallas kernels: 139 us -> 137 us
    pallas_call x1, Pallas kernels: 139 us -> 137 us  [right_side_of(): pl.pallas_call(kernel, out_shape=jax.ShapeDtypeStruct((XL, YL, NZ), BF16)...]
where the time goes in v4:
time: 144 us
  Pallas kernels  137 us (95%)
  matrix products  5.36 us (4%)
    pallas_call x1, Pallas kernels, right_side_of(): pl.pallas_call(kernel, out_shape=jax.ShapeDtypeStruct((XL, YL, NZ), BF16)...  137 us
    dot_general x1, matrix products, per_device(): jnp.einsum('xyin,xaybn->xaybi', inverse_blocks, grouped, preferred_elemen...  5.36 us

profile of v4, /device:TPU:1, one launch (start us, length us, event | category | flops | bytes accessed | tf_op | source)
XLA Modules:
  0.0 143.7 jit_solution(16159872734675498382)
XLA Ops:
  0.0 0.0 copy-start
  0.0 137.2 %spectral.1 = bf16[16,64,128]{2,1,0:T(8,128)(2,1)} custom-call(f32[16,64,128]{2,1,0:T(8,128)} %vx_hbm.1, f32[16,64,128]{2,1,0:T(8,128)} %vy_hbm.1, f32[16,64,128]{2,1,0:T(8,128)} %vz_hbm.1, f32[16,64,128]{2,1,0:T(8,128)} %b_hbm.1, bf16[2,192,128]{2,1,0:T(8,128)(2,1)} %constant.12.clone.zf_hbm, bf16[2,256,256]{2,1,0:T(8,128)(2,1)} %constant.17.clone.zb_hbm, ...), custom_call_target="tpu_custom_call" | custom-call | tf_op jit(solution)/shard_map/spectral/pallas_call | solution.py:364
  137.3 0.0 copy-done
  137.3 5.4 %fusion.2 = f32[8,2,32,2,128]{4,3,1,2,0:T(2,128)S(1)} fusion(bf16[8,32,128,128]{3,2,1,0:T(8,128)(2,1)S(1)} %copy-done, bf16[8,2,32,2,128]{4,3,2,1,0:T(2,128)(2,1)} %bitcast.11), kind=kOutput, calls=%fused_computation.2 | convolution fusion | flops 33554432 | bytes 9175040 | tf_op jit(solution)/shard_map/xyin,xaybn->xaybi/dot_general | solution.py:380
  142.6 1.0 copy.14
Async XLA Ops:
  0.0 137.3 %copy-start = (bf16[8,32,128,128]{3,2,1,0:T(8,128)(2,1)S(1)}, bf16[8,32,128,128]{3,2,1,0:T(8,128)(2,1)}, u32[]{:S(2)}) copy-start(bf16[8,32,128,128]{3,2,1,0:T(8,128)(2,1)} %param.15) | copy-start | bytes 25165828

commit v5 on v4

--- a/solution.py
+++ b/solution.py
@@ -102,7 +102,7 @@
     out_ref,
     send1, recv1, send2, recv2, send3, recv3, send4, recv4,
     vx_ref, vy_ref, vz_ref, b_ref, zf, zb, xf, yf, yb, xb,
-    xh, xl, yh, yl, gh, gl, bh, bl, zh, zl,
+    xh, xl, yh, yl, gh, gl, bh, bl, zh, zl, partial,
     table_sem, s1, r1, s2, r2, s3, r3, s4, r4,
 ):
     w = lax.axis_index("wide")
@@ -323,17 +323,30 @@
 
     zh[...] = jnp.zeros_like(zh)
     zl[...] = jnp.zeros_like(zl)
-    for c in range(QL):
+    early = 4 * W
+
+    def z_rows(i, start, size):
+        for side in range(2):
+            high, low = halves(recv4[0, pl.ds(start * XL + 2 * i + side, size, stride=XL), :])
+            zh[start : start + size, side * 128 : (side + 1) * 128] = high
+            zl[start : start + size, side * 128 : (side + 1) * 128] = low
+
+    for c in range(4):
+        wait(recv4, c, NX, r4)
+
+    @pl.loop(0, XL // 2)
+    def _(i):
+        z_rows(i, 0, early)
+        partial[i] = dot3(zb[0, :, :early], zb[1, :, :early], zh[:early, :], zl[:early, :])
+
+    for c in range(4, QL):
         wait(recv4, c, NX, r4)
     wide_lanes = lax.broadcasted_iota(jnp.int32, (NZ, 128), 1) < 64
 
     @pl.loop(0, XL // 2)
     def _(i):
-        for side in range(2):
-            high, low = halves(recv4[0, pl.ds(2 * i + side, MZ, stride=XL), :])
-            zh[:MZ, side * 128 : (side + 1) * 128] = high
-            zl[:MZ, side * 128 : (side + 1) * 128] = low
-        value = dot3(zb[0], zb[1], zh[...], zl[...])
+        z_rows(i, early, MZ - early)
+        value = partial[i] + dot3(zb[0, :, early:], zb[1, :, early:], zh[early:, :], zl[early:, :])
         first = value[:NZ, :128] + pltpu.roll(value[NZ:, :128], 64, 1)
         second = pltpu.roll(value[:NZ, 128:], 64, 1) + value[NZ:, 128:]
         nonlinear = jnp.where(wide_lanes, first, second).T
@@ -360,6 +373,7 @@
     split = []
     for shape in ((NX, 256), (4 * PL, NY), (3 * PL, MY), (MX, 256), (256, 256)):
         split += [pltpu.VMEM(shape, BF16)] * 2
+    split.append(pltpu.VMEM((XL // 2, 2 * NZ, 256), F32))
     sems = [pltpu.SemaphoreType.DMA((count,)) for count in (10,) + (QL,) * 8]
     return pl.pallas_call(
         kernel,

time: 144 us -> 143 us (level)
  no operation moved by 1% of the time
where the time goes in v5:
time: 143 us
  Pallas kernels  137 us (96%)
  matrix products  5.36 us (4%)
    pallas_call x1, Pallas kernels, right_side_of(): pl.pallas_call(kernel, out_shape=jax.ShapeDtypeStruct((XL, YL, NZ), BF16)...  137 us
    dot_general x1, matrix products, per_device(): jnp.einsum('xyin,xaybn->xaybi', inverse_blocks, grouped, preferred_elemen...  5.36 us

profile of v5, /device:TPU:1, one launch (start us, length us, event | category | flops | bytes accessed | tf_op | source)
XLA Modules:
  0.0 143.2 jit_solution(6370050020986006222)
XLA Ops:
  0.0 0.0 copy-start
  0.0 136.7 %spectral.1 = bf16[16,64,128]{2,1,0:T(8,128)(2,1)} custom-call(f32[16,64,128]{2,1,0:T(8,128)} %vx_hbm.1, f32[16,64,128]{2,1,0:T(8,128)} %vy_hbm.1, f32[16,64,128]{2,1,0:T(8,128)} %vz_hbm.1, f32[16,64,128]{2,1,0:T(8,128)} %b_hbm.1, bf16[2,192,128]{2,1,0:T(8,128)(2,1)} %constant.12.clone.zf_hbm, bf16[2,256,256]{2,1,0:T(8,128)(2,1)} %constant.17.clone.zb_hbm, ...), custom_call_target="tpu_custom_call" | custom-call | tf_op jit(solution)/shard_map/spectral/pallas_call | solution.py:378
  136.7 0.0 copy-done
  136.8 5.4 %fusion.2 = f32[8,2,32,2,128]{4,3,1,2,0:T(2,128)S(1)} fusion(bf16[8,32,128,128]{3,2,1,0:T(8,128)(2,1)S(1)} %copy-done, bf16[8,2,32,2,128]{4,3,2,1,0:T(2,128)(2,1)} %bitcast.11), kind=kOutput, calls=%fused_computation.2 | convolution fusion | flops 33554432 | bytes 9175040 | tf_op jit(solution)/shard_map/xyin,xaybn->xaybi/dot_general | solution.py:394
  142.1 1.0 copy.14
Async XLA Ops:
  0.0 136.7 %copy-start = (bf16[8,32,128,128]{3,2,1,0:T(8,128)(2,1)S(1)}, bf16[8,32,128,128]{3,2,1,0:T(8,128)(2,1)}, u32[]{:S(2)}) copy-start(bf16[8,32,128,128]{3,2,1,0:T(8,128)(2,1)} %param.15) | copy-start | bytes 25165828
